TPU v7x, 256 devices: a whole 4x4x8 slice. The times are simulated.
256 devices in a mesh: dp: 16 (over z, core), mp: 16 (over x, y).
Axes of the slice: x: 4, y: 4, z: 8, core: 2. Of those that a mesh axis runs over, the one named last changes fastest.
Arguments:
- hidden_in: bfloat16 [64, 64, 7168], P('dp', None, 'mp'), may hold values from -6 to 6
- norm_gain: bfloat16 [7168], P('mp'), may hold values from 0.099609375 to 1.8984375
- w_query: bfloat16 [7168, 7168], P('dp', 'mp'), may hold values from -0.070868339 to 0.070868339
- w_key: bfloat16 [7168, 1024], P('dp', 'mp'), may hold values from -0.070868339 to 0.070868339
- w_value: bfloat16 [7168, 1024], P('dp', 'mp'), may hold values from -0.0625 to 0.0625
- w_out: bfloat16 [7168, 7168], P('mp', 'dp'), may hold values from -0.09375 to 0.09375
- key_cache: bfloat16 [64, 16, 1, 2048, 128], P('dp', 'mp'), may hold values from -52 to 52
- value_cache: bfloat16 [64, 16, 1, 2048, 128], P('dp', 'mp'), may hold values from -3 to 3
- cache_len: int32 [64], P('dp'), may hold values from 256 to 4096, as said below
- tree_parent: int32 [64, 64], P('dp'), may hold values from 0 to 62, as said below
- valid_nodes: int32 [64, 64], P('dp'), may hold values from 0 to 1, as said below
- accepted_path: int32 [64, 8], P('dp'), may hold values from 0 to 63, as said below
- slot_owner: int32 [64], replicated, may hold values from 0 to 63, each once
Outputs:
- layer_out: bfloat16 [64, 64, 7168], P('dp', None, 'mp')
- accepted_kv: bfloat16 [64, 8, 2, 1024], P('dp', None, None, 'mp')
Inputs may be any that keep to these rules, and one draw needn't show every extreme that they name: `cache_len`: some request holds exactly 4096 positions in every draw. `tree_parent`: node 0 is its own parent; every other node's parent is one of the three nodes before it. `valid_nodes`: the 1 entries of each request form a prefix of 32 to 64 nodes. `accepted_path`: each row is a chain in which every node is the parent of the next (node 0 may repeat at the start), ending at the request's last real node. `slot_owner`: each slot is named once.
All inputs are finite; a program needn't handle non-finite values.
Results may differ from a plain program's by a relative error of at most 0.007.
The roundings to bfloat16 on the way count: a program that leaves them out, or rounds other values in their place, can miss the bound.
Values may be sent and summed in bfloat16 or wider, within the bound.
No kernel may reach another device: no remote copies, remote signals or barrier semaphores. Data moves between devices by JAX's collectives and lax.ppermute only.
A program may use at most 128 MiB of HBM per device.

v0:
```python
import math
import jax
import jax.numpy as jnp
from jax import lax
from jax.sharding import PartitionSpec as P

GROUP = 7
epsilon = 1e-05
rope_base = 5000000.0
masked_score = -1e30


def from_partner(block, axis, stride):
    count = lax.axis_size(axis)
    route = []
    for low in range(count):
        high = low | 1 << stride
        if high != low and high < count:
            route += [(low, high), (high, low)]
    return lax.ppermute(block, axis, route)


def tree_closure(parents):
    width = parents.shape[-1]
    nodes = jnp.arange(width, dtype=jnp.int32)
    onehot = (parents[..., None] == nodes).astype(jnp.float32)
    reach = jnp.minimum(jnp.eye(width, dtype=jnp.float32) + onehot, 1.0)
    for rounds in range((width - 1).bit_length()):
        reach = jnp.minimum(
            jnp.einsum("rij,rjk->rik", reach, reach, precision=lax.Precision.HIGHEST), 1.0
        )
    return reach


def rotate(values, positions):
    head_dim = values.shape[-1]
    half_dim = head_dim // 2
    freq_steps = jnp.arange(half_dim, dtype=jnp.float32)
    inverse = jnp.exp(freq_steps * (-2.0 * math.log(rope_base) / head_dim))
    angles = positions[..., None] * inverse
    cosine = jnp.concatenate([jnp.cos(angles), jnp.cos(angles)], -1)[..., None, :]
    sine = jnp.concatenate([jnp.sin(angles), jnp.sin(angles)], -1)[..., None, :]
    turned = jnp.concatenate([-values[..., half_dim:], values[..., :half_dim]], -1)
    return values * cosine + turned * sine


def shards(
    hidden_in,
    norm_gain,
    w_query,
    w_key,
    w_value,
    w_out,
    key_cache,
    value_cache,
    cache_len,
    tree_parent,
    valid_nodes,
    accepted_path,
    slot_owner,
):
    req_dev, tree_size, part_width = hidden_in.shape
    row_count = req_dev * tree_size
    head_dim = key_cache.shape[-1]
    half_len = key_cache.shape[3]
    kv_group = key_cache.shape[2]
    q_cols = w_query.shape[1]
    k_cols = w_key.shape[1]
    gathered, full_gain = (
        lax.all_gather(hidden_in, "mp", axis=2, tiled=True),
        lax.all_gather(norm_gain, "mp", axis=0, tiled=True),
    )
    widened = gathered.astype(jnp.float32)
    meansq = jnp.mean(widened * widened, -1, keepdims=True)
    normed = (widened * lax.rsqrt(meansq + epsilon) * full_gain.astype(jnp.float32)).astype(
        jnp.bfloat16
    )
    flat = normed.reshape(row_count, gathered.shape[2])
    pieces = (
        lax.all_gather(w_query, "dp", axis=0, tiled=True),
        lax.all_gather(w_key, "dp", axis=0, tiled=True),
        lax.all_gather(w_value, "dp", axis=0, tiled=True),
    )
    query_sum, key_sum, value_sum = tuple(
        (jnp.dot(flat, piece, preferred_element_type=jnp.float32) for piece in pieces)
    )
    query = query_sum.astype(jnp.bfloat16)
    key_new = key_sum.astype(jnp.bfloat16)
    value_new = value_sum.astype(jnp.bfloat16)
    other_query, other_key, other_value = from_partner((query, key_new, value_new), "mp", 0)
    half_index = lax.axis_index("mp") % 2
    is_first = half_index == 0

    def paired(own_part, other_part):
        return jnp.where(
            is_first,
            jnp.concatenate([own_part, other_part], 1),
            jnp.concatenate([other_part, own_part], 1),
        )

    group_query = paired(query, other_query)
    group_key = paired(key_new, other_key)
    group_value = paired(value_new, other_value)
    reach = tree_closure(tree_parent)
    depth = jnp.sum(reach, -1) - 1.0
    position = cache_len[:, None].astype(jnp.float32) + depth
    rot_query = rotate(
        group_query.reshape(req_dev, tree_size, kv_group * GROUP, head_dim).astype(jnp.float32),
        position,
    ).astype(jnp.bfloat16)
    rot_key = rotate(
        group_key.reshape(req_dev, tree_size, kv_group, head_dim).astype(jnp.float32), position
    ).astype(jnp.bfloat16)
    node_values = group_value.reshape(req_dev, tree_size, kv_group, head_dim)
    queries_all = (
        rot_query.reshape(req_dev, tree_size, kv_group, GROUP, head_dim)
        .transpose(0, 2, 3, 1, 4)
        .reshape(req_dev, kv_group, GROUP * tree_size, head_dim)
    )
    scale = 1.0 / math.sqrt(head_dim)

    def one_request(packed):
        queries, key_r, value_r, cached_keys, cached_values, length, reach_r = packed
        tree_keys = key_r.transpose(1, 0, 2)
        tree_values = value_r.transpose(1, 0, 2)
        count = jnp.clip(length - half_index * half_len, 0, half_len)
        scores_tree = (
            jnp.einsum("gqd,gkd->gqk", queries, tree_keys, preferred_element_type=jnp.float32)
            * scale
        )
        tiled = jnp.logical_and(jnp.tile(reach_r, (GROUP, 1)) > 0.5, is_first)
        scores_tree = jnp.where(tiled[None], scores_tree, masked_score)
        scores_cache = (
            jnp.einsum("gqd,gkd->gqk", queries, cached_keys, preferred_element_type=jnp.float32)
            * scale
        )
        live = jnp.arange(half_len, dtype=jnp.int32) < count
        scores_cache = jnp.where(live[None, None, :], scores_cache, masked_score)
        highest = jnp.maximum(jnp.max(scores_cache, -1), jnp.max(scores_tree, -1))
        probs_cache = jnp.exp(scores_cache - highest[..., None]).astype(jnp.bfloat16)
        probs_tree = jnp.exp(scores_tree - highest[..., None]).astype(jnp.bfloat16)
        totals = jnp.sum(probs_cache.astype(jnp.float32), -1) + jnp.sum(
            probs_tree.astype(jnp.float32), -1
        )
        weighted = jnp.einsum(
            "gqk,gkd->gqd", probs_cache, cached_values, preferred_element_type=jnp.float32
        )
        weighted = weighted + jnp.einsum(
            "gqk,gkd->gqd", probs_tree, tree_values, preferred_element_type=jnp.float32
        )
        return (highest, totals, weighted)

    highest, totals, weighted = lax.map(
        one_request,
        (queries_all, rot_key, node_values, key_cache[:, 0], value_cache[:, 0], cache_len, reach),
    )
    other_high, other_totals, other_weighted = from_partner((highest, totals, weighted), "mp", 0)
    ceiling = jnp.maximum(highest, other_high)
    own_factor = jnp.exp(highest - ceiling)
    other_factor = jnp.exp(other_high - ceiling)
    numerator = weighted * own_factor[..., None] + other_weighted * other_factor[..., None]
    denominator = totals * own_factor + other_totals * other_factor
    attended = (numerator / denominator[..., None]).astype(jnp.bfloat16)
    attended = (
        attended.reshape(req_dev, kv_group, GROUP, tree_size, head_dim)
        .transpose(0, 3, 1, 2, 4)
        .reshape(req_dev, tree_size, kv_group * GROUP * head_dim)
    )
    attended = attended * valid_nodes[..., None].astype(jnp.bfloat16)
    own_heads = lax.dynamic_slice_in_dim(
        attended.reshape(row_count, 2 * q_cols), half_index * q_cols, q_cols, 1
    )
    terms = jnp.dot(
        own_heads,
        lax.all_gather(w_out, "dp", axis=1, tiled=True),
        preferred_element_type=jnp.float32,
    )
    mine = lax.psum_scatter(terms, "mp", scatter_dimension=1, tiled=True)
    layer_out = (
        (hidden_in.reshape(row_count, part_width).astype(jnp.float32) + mine)
        .astype(jnp.bfloat16)
        .reshape(req_dev, tree_size, part_width)
    )
    own_keys = lax.dynamic_slice_in_dim(
        rot_key.reshape(req_dev, tree_size, kv_group * head_dim), half_index * k_cols, k_cols, 2
    )
    kv_rows = jnp.stack([own_keys, value_new.reshape(req_dev, tree_size, k_cols)], 2)
    chosen = jax.vmap(lambda rows_of, picks: jnp.take(rows_of, picks, axis=0))(
        kv_rows, accepted_path
    )
    every_row = lax.all_gather(chosen, "dp", axis=0, tiled=True)
    total_reqs = slot_owner.shape[0]
    my_slots = lax.axis_index("dp") * req_dev + jnp.arange(req_dev, dtype=jnp.int32)
    matches = slot_owner[None, :] == my_slots[:, None]
    senders = jnp.sum(jnp.where(matches, jnp.arange(total_reqs, dtype=jnp.int32)[None, :], 0), 1)
    accepted_kv = jnp.take(every_row, senders, axis=0)
    return (layer_out, accepted_kv)


def solution(mesh):
    placed = (
        P("dp", None, "mp"),
        P("mp"),
        P("dp", "mp"),
        P("dp", "mp"),
        P("dp", "mp"),
        P("mp", "dp"),
        P("dp", "mp", None, None, None),
        P("dp", "mp", None, None, None),
        P("dp"),
        P("dp", None),
        P("dp", None),
        P("dp", None),
        P(),
    )
    return jax.shard_map(
        shards,
        mesh=mesh,
        in_specs=placed,
        out_specs=(P("dp", None, "mp"), P("dp", None, None, "mp")),
        check_vma=False,
    )
```

profile of v0, /device:TPU:2, one launch (start us, length us, event | category | flops | bytes accessed | tf_op | source)
XLA Modules:
  0.0 352.2 jit_solution(6628368691060993493)
XLA Ops:
  7.2 2.0 copy.134
  9.3 0.7 all-gather.8.cloned.1.call-update
  10.1 2.0 copy.158
  12.2 1.3 dynamic-slice.1
  14.1 0.9 dynamic-update-slice
  15.0 69.3 %all-reduce = bf16[7168]{0:T(1024)(128)(2,1)S(1)} all-reduce(bf16[7168]{0:T(1024)(128)(2,1)S(1)} %dynamic-update-slice), channel_id=1, replica_groups=mesh['dp'=16,'mp'=16] {'mp'}, use_global_device_ids=true, to_apply=%add | all-reduce | flops 7168 | bytes 28672
  84.3 26.0 %all-gather = bf16[16,448,64]{1,2,0:T(8,128)(2,1)S(1)} all-gather(bf16[1,448,64]{1,2,0:T(8,128)(2,1)} %bitcast.153), channel_id=1, replica_groups=mesh['dp'=16,'mp'=16] {'dp'}, dimensions={0}, use_global_device_ids=true | all-gather | bytes 974848 | tf_op jit(solution)/shard_map/all_gather | solution.py:81
  110.4 0.6 copy.141
  110.9 1.2 reshape.579
  112.1 0.4 convolution_minimum_fusion.5
  114.0 24.1 %all-gather.1 = bf16[16,448,64]{1,2,0:T(8,128)(2,1)S(1)} all-gather(bf16[1,448,64]{1,2,0:T(8,128)(2,1)S(1)} %bitcast.154), channel_id=1, replica_groups=mesh['dp'=16,'mp'=16] {'dp'}, dimensions={0}, use_global_device_ids=true | all-gather | bytes 974848 | tf_op jit(solution)/shard_map/all_gather | solution.py:82
  138.1 0.6 copy.148
  138.6 1.2 reshape.581
  139.9 0.5 fusion.42
  140.4 0.8 pad_maximum_fusion
  141.2 11.3 %copy.135 = bf16[4,64,7168]{2,1,0:T(8,128)(2,1)} copy(bf16[4,64,7168]{1,0,2:T(4,128)(2,1)} %all-gather.6.cloned.1.call-done) | data formatting | bytes 7340032 | tf_op jit(solution)/shard_map/all_gather | solution.py:70
  152.5 3.0 fusion.22
  155.7 1.0 fusion.24
  156.7 1.2 convolution_convert_fusion.2
  158.1 0.5 copy-done.1
  158.6 1.2 convolution_convert_fusion.1
  160.0 1.8 collective-permute-start.2
  162.5 7.2 %convolution_convert_fusion = bf16[256,448]{0,1:T(8,128)(2,1)S(1)} fusion(bf16[256,7168]{1,0:T(8,128)(2,1)} %bitcast.138, bf16[7168,448]{1,0:T(8,128)(2,1)} %all-gather.8.cloned.1.call-done), kind=kOutput, calls=%fused_computation.41 | convolution fusion | flops 1644281856 | bytes 10321920 | tf_op jit(solution)/shard_map/dot_general | solution.py:85
  169.7 0.6 collective-permute-start
  170.3 0.4 fusion.36
  170.8 0.7 fusion.38
  171.6 5.6 %collective-permute-done = bf16[256,448]{0,1:T(8,128)(2,1)S(1)} collective-permute-done((bf16[256,448]{0,1:T(8,128)(2,1)S(1)}, bf16[256,448]{0,1:T(8,128)(2,1)S(1)}, u32[]{:S(2)}, u32[]{:S(2)}) %collective-permute-start) | collective-permute-done | bytes 229408 | tf_op jit(solution)/shard_map/ppermute | solution.py:20
  178.2 0.5 copy-done.5
  178.7 0.5 fusion.28
  179.3 42.3 %while.16 = (s32[]{:T(128)}, f32[4,1,448]{2,1,0:T(1,128)S(1)}, f32[4,1,448]{2,1,0:T(1,128)S(1)}, f32[4,1,448,128]{3,2,1,0:T(8,128)S(1)}, s32[4]{0:T(128)S(1)}, /...) while((s32[]{:T(128)}, f32[4,1,448]{2,1,0:T(1,128)S(1)}, ...), condition=%wide.region_7.8_spmd, body=%wide.region_2.7_spmd.sunk | while | flops 496694400 | bytes 28287568 | solution.py:153
  179.3 0.6 dynamic_slice.100
  180.6 3.6 %fusion.79 = (f32[448]{0:T(512)S(1)}, f32[448,2048]{1,0:T(8,128)}) fusion(pred[2048]{0:T(1024)(128)(4,1)S(1)} %iota_compare_fusion.5, bf16[4,1,2048,128]{3,2,1,0:T(8,128)(2,1)} %get-tuple-element.394, s32[]{:T(128)} %get-tuple-element.371, bf16[4,1,448,128]{3,2,1,0:T(8,128)(2,1)S(1)} %get-tuple-element.393), kind=kOutput, calls=%fused_computation.5.clone.1 | convolution fusion | flops 237633088 | bytes 4313856 | tf_op jit(solution)/shard_map/while/body/eval_jaxpr/gqd,gkd->gqk/dot_general | solution.py:134
  184.8 1.1 fusion.81
  185.9 3.1 fusion.82
  189.1 0.8 convert_reduce_fusion.4
  190.0 0.6 dynamic_slice.100
  191.2 3.6 %fusion.79 = (f32[448]{0:T(512)S(1)}, f32[448,2048]{1,0:T(8,128)}) fusion(pred[2048]{0:T(1024)(128)(4,1)S(1)} %iota_compare_fusion.5, bf16[4,1,2048,128]{3,2,1,0:T(8,128)(2,1)} %get-tuple-element.394, s32[]{:T(128)} %get-tuple-element.371, bf16[4,1,448,128]{3,2,1,0:T(8,128)(2,1)S(1)} %get-tuple-element.393), kind=kOutput, calls=%fused_computation.5.clone.1 | convolution fusion | flops 237633088 | bytes 4313856 | tf_op jit(solution)/shard_map/while/body/eval_jaxpr/gqd,gkd->gqk/dot_general | solution.py:134
  195.4 1.1 fusion.81
  196.5 3.1 fusion.82
  199.6 0.8 convert_reduce_fusion.4
  200.5 0.6 dynamic_slice.100
  201.8 3.6 %fusion.79 = (f32[448]{0:T(512)S(1)}, f32[448,2048]{1,0:T(8,128)}) fusion(pred[2048]{0:T(1024)(128)(4,1)S(1)} %iota_compare_fusion.5, bf16[4,1,2048,128]{3,2,1,0:T(8,128)(2,1)} %get-tuple-element.394, s32[]{:T(128)} %get-tuple-element.371, bf16[4,1,448,128]{3,2,1,0:T(8,128)(2,1)S(1)} %get-tuple-element.393), kind=kOutput, calls=%fused_computation.5.clone.1 | convolution fusion | flops 237633088 | bytes 4313856 | tf_op jit(solution)/shard_map/while/body/eval_jaxpr/gqd,gkd->gqk/dot_general | solution.py:134
  205.9 1.1 fusion.81
  207.1 3.1 fusion.82
  210.2 0.8 convert_reduce_fusion.4
  211.1 0.6 dynamic_slice.100
  212.3 3.6 %fusion.79 = (f32[448]{0:T(512)S(1)}, f32[448,2048]{1,0:T(8,128)}) fusion(pred[2048]{0:T(1024)(128)(4,1)S(1)} %iota_compare_fusion.5, bf16[4,1,2048,128]{3,2,1,0:T(8,128)(2,1)} %get-tuple-element.394, s32[]{:T(128)} %get-tuple-element.371, bf16[4,1,448,128]{3,2,1,0:T(8,128)(2,1)S(1)} %get-tuple-element.393), kind=kOutput, calls=%fused_computation.5.clone.1 | convolution fusion | flops 237633088 | bytes 4313856 | tf_op jit(solution)/shard_map/while/body/eval_jaxpr/gqd,gkd->gqk/dot_general | solution.py:134
  216.5 1.1 fusion.81
  217.6 3.1 fusion.82
  220.7 0.8 convert_reduce_fusion.4
  221.6 0.8 collective-permute-start.4
  222.5 1.3 collective-permute-start.3
  223.7 0.8 collective-permute-start.5
  224.6 18.7 %collective-permute-done.3 = f32[4,1,448]{2,1,0:T(1,128)S(1)} collective-permute-done((f32[4,1,448]{2,1,0:T(1,128)S(1)}, f32[4,1,448]{2,1,0:T(1,128)S(1)}, u32[]{:S(2)}, u32[]{:S(2)}) %collective-permute-start.3) | collective-permute-done | bytes 7200 | tf_op jit(solution)/shard_map/ppermute | solution.py:20
  243.5 0.9 divide_convert_fusion
  244.8 8.3 %fusion.30 = f32[256,7168]{0,1:T(8,128)} fusion(bf16[448,7168]{0,1:T(8,128)(2,1)} %all-gather.10.cloned.1.call-done, bf16[256,896]{1,0:T(8,128)(2,1)S(1)} %bitcast.145, s32[]{:T(128)S(6)} %select_n.115, bf16[256]{0:T(256)(128)(2,1)S(1)} %mul.204), kind=kOutput, calls=%fused_computation.63 | convolution fusion | flops 1644625920 | bytes 14025220 | tf_op jit(solution)/shard_map/dot_general | solution.py:173
  253.1 0.9 copy-done.3
  255.4 0.7 gather_fusion.1
  256.1 16.2 %all_gather.27 = bf16[64,8,2,64]{3,1,2,0:T(8,128)(2,1)S(1)} all-gather(bf16[4,8,2,64]{3,1,2,0:T(8,128)(2,1)S(1)} %copy_select_fusion), channel_id=1, replica_groups=mesh['dp'=16,'mp'=16] {'dp'}, dimensions={0}, use_global_device_ids=true | all-gather | bytes 139264 | tf_op jit(solution)/shard_map/all_gather | solution.py:191
  272.3 0.6 gather_fusion
  272.9 0.6 copy.163
  273.6 70.2 %reduce-scatter.2.cloned.1.call-done = f32[256,448]{0,1:T(8,128)} async-done(((f32[256,7168]{0,1:T(8,128)}), f32[256,448]{0,1:T(8,128)}) %reduce-scatter.2.cloned.1.call-update) | async-done | bytes 458768 | tf_op jit(solution)/shard_map/reduce_scatter | solution.py:178
  343.7 1.1 add_convert_fusion
  344.8 0.8 copy.160
  (149 shorter events, 8.5 us)
Async XLA Ops:
  7.2 134.1 %all-gather.6.cloned.1.call-start = ((), (), s32[]{:S(2)}) async-start(), calls=%async_computation.1 | async-start | bytes 7798784 | tf_op jit(solution)/shard_map/all_gather | solution.py:70
  9.3 102.9 %copy-start.9 = (s32[4,64]{1,0:T(4,128)S(1)}, s32[4,64]{1,0:T(4,128)}, u32[]{:S(2)}) copy-start(s32[4,64]{1,0:T(4,128)} %param.24) | copy-start | bytes 3076
  9.3 153.2 %all-gather.8.cloned.1.call-start = ((), (), s32[]{:S(2)}) async-start(), calls=%async_computation.2 | async-start | bytes 7798784 | tf_op jit(solution)/shard_map/all_gather | solution.py:80
  10.0 234.8 %all-gather.10.cloned.1.call-start = ((), (), s32[]{:S(2)}) async-start(), calls=%async_computation.3 | async-start | bytes 7798784 | tf_op jit(solution)/shard_map/all_gather | solution.py:175
  12.1 331.7 %reduce-scatter.2.cloned.1.call-start = ((), (), s32[]{:S(2)}) async-start(), calls=%async_computation.4 | async-start | bytes 7798784 | tf_op jit(solution)/shard_map/reduce_scatter | solution.py:178
  84.3 29.6 %copy-start.10 = (s32[4]{0:T(128)S(1)}, s32[4]{0:T(128)}, u32[]{:S(2)}) copy-start(s32[4]{0:T(128)} %param.23) | copy-start | bytes 52
  84.3 29.6 %copy-start.6 = (bf16[448,64]{0,1:T(8,128)(2,1)S(1)}, bf16[448,64]{0,1:T(8,128)(2,1)}, u32[]{:S(2)}) copy-start(bf16[448,64]{0,1:T(8,128)(2,1)} %param.19) | copy-start | bytes 172036
  152.5 3.1 copy-start.2
  156.7 1.8 copy-start.1
  158.0 4.0 %collective-permute-start.1 = (bf16[256,64]{0,1:T(8,128)(2,1)S(1)}, bf16[256,64]{0,1:T(8,128)(2,1)S(1)}, u32[]{:S(2)}, u32[]{:S(2)}) collective-permute-start(bf16[256,64]{0,1:T(8,128)(2,1)S(1)} %convolution_convert_fusion.2), channel_id=1, source_target_pairs={{0,1},{1,0},{2,3},{3,2},{4,5},{5,4},{6,7},{7,6},{8,9},{9,8},{10,11... | collective-permute-start | bytes 98312 | tf_op jit(solution)/shard_map/ppermute | solution.py:20
  160.0 10.7 %collective-permute-start.2 = (bf16[256,64]{0,1:T(8,128)(2,1)S(1)}, bf16[256,64]{0,1:T(8,128)(2,1)S(1)}, u32[]{:S(2)}, u32[]{:S(2)}) collective-permute-start(bf16[256,64]{0,1:T(8,128)(2,1)S(1)} %convolution_convert_fusion.1), channel_id=1, source_target_pairs={{0,1},{1,0},{2,3},{3,2},{4,5},{5,4},{6,7},{7,6},{8,9},{9,8},{10,11... | collective-permute-start | bytes 98312 | tf_op jit(solution)/shard_map/ppermute | solution.py:20
  169.7 7.4 %collective-permute-start = (bf16[256,448]{0,1:T(8,128)(2,1)S(1)}, bf16[256,448]{0,1:T(8,128)(2,1)S(1)}, u32[]{:S(2)}, u32[]{:S(2)}) collective-permute-start(bf16[256,448]{0,1:T(8,128)(2,1)S(1)} %convolution_convert_fusion), channel_id=1, source_target_pairs={{0,1},{1,0},{2,3},{3,2},{4,5},{5,4},{6,7},{7,6},{8,9},{9,8},{10,11... | collective-permute-start | bytes 688136 | tf_op jit(solution)/shard_map/ppermute | solution.py:20
  177.8 0.9 copy-start.5
  177.8 1.5 copy-start.4
  178.2 1.1 copy-start.11
  179.3 45.2 %copy-start.8 = (s32[4,64]{1,0:T(4,128)S(1)}, s32[4,64]{1,0:T(4,128)}, u32[]{:S(2)}) copy-start(s32[4,64]{1,0:T(4,128)} %param.25) | copy-start | bytes 3076
  184.5 4.5 %copy-start = (f32[448,2048]{1,0:T(8,128)S(1)}, f32[448,2048]{1,0:T(8,128)}, u32[]{:S(2)}) copy-start(f32[448,2048]{1,0:T(8,128)} %get-tuple-element.351) | copy-start | bytes 11010052 | tf_op jit(solution)/shard_map/while
  185.9 4.1 %copy-start.12 = (s32[4]{0:T(128)S(1)}, s32[4]{0:T(128)}, u32[]{:S(2)}) copy-start(s32[4]{0:T(128)} %get-tuple-element.447) | copy-start | bytes 52 | tf_op jit(solution)/shard_map/while
  195.2 4.5 %copy-start = (f32[448,2048]{1,0:T(8,128)S(1)}, f32[448,2048]{1,0:T(8,128)}, u32[]{:S(2)}) copy-start(f32[448,2048]{1,0:T(8,128)} %get-tuple-element.351) | copy-start | bytes 11010052 | tf_op jit(solution)/shard_map/while
  196.5 4.0 %copy-start.12 = (s32[4]{0:T(128)S(1)}, s32[4]{0:T(128)}, u32[]{:S(2)}) copy-start(s32[4]{0:T(128)} %get-tuple-element.447) | copy-start | bytes 52 | tf_op jit(solution)/shard_map/while
  205.7 4.5 %copy-start = (f32[448,2048]{1,0:T(8,128)S(1)}, f32[448,2048]{1,0:T(8,128)}, u32[]{:S(2)}) copy-start(f32[448,2048]{1,0:T(8,128)} %get-tuple-element.351) | copy-start | bytes 11010052 | tf_op jit(solution)/shard_map/while
  207.0 4.0 %copy-start.12 = (s32[4]{0:T(128)S(1)}, s32[4]{0:T(128)}, u32[]{:S(2)}) copy-start(s32[4]{0:T(128)} %get-tuple-element.447) | copy-start | bytes 52 | tf_op jit(solution)/shard_map/while
  216.3 4.5 %copy-start = (f32[448,2048]{1,0:T(8,128)S(1)}, f32[448,2048]{1,0:T(8,128)}, u32[]{:S(2)}) copy-start(f32[448,2048]{1,0:T(8,128)} %get-tuple-element.351) | copy-start | bytes 11010052 | tf_op jit(solution)/shard_map/while
  217.6 4.0 %copy-start.12 = (s32[4]{0:T(128)S(1)}, s32[4]{0:T(128)}, u32[]{:S(2)}) copy-start(s32[4]{0:T(128)} %get-tuple-element.447) | copy-start | bytes 52 | tf_op jit(solution)/shard_map/while
  221.6 21.8 %collective-permute-start.4 = (f32[4,1,448,128]{3,2,1,0:T(8,128)S(1)}, f32[4,1,448,128]{3,2,1,0:T(8,128)S(1)}, u32[]{:S(2)}, u32[]{:S(2)}) collective-permute-start(f32[4,1,448,128]{3,2,1,0:T(8,128)S(1)} %get-tuple-element.434), channel_id=1, source_target_pairs={{0,1},{1,0},{2,3},{3,2},{4,5},{5,4},{6,7},{7,6},{8,9},{9,8},{10,11... | collective-permute-start | bytes 2752520 | tf_op jit(solution)/shard_map/ppermute | solution.py:20
  222.5 20.8 %collective-permute-start.3 = (f32[4,1,448]{2,1,0:T(1,128)S(1)}, f32[4,1,448]{2,1,0:T(1,128)S(1)}, u32[]{:S(2)}, u32[]{:S(2)}) collective-permute-start(f32[4,1,448]{2,1,0:T(1,128)S(1)} %get-tuple-element.432), channel_id=1, source_target_pairs={{0,1},{1,0},{2,3},{3,2},{4,5},{5,4},{6,7},{7,6},{8,9},{9,8},{10,11... | collective-permute-start | bytes 21512 | tf_op jit(solution)/shard_map/ppermute | solution.py:20
  223.7 19.6 %collective-permute-start.5 = (f32[4,1,448]{2,1,0:T(1,128)S(1)}, f32[4,1,448]{2,1,0:T(1,128)S(1)}, u32[]{:S(2)}, u32[]{:S(2)}) collective-permute-start(f32[4,1,448]{2,1,0:T(1,128)S(1)} %get-tuple-element.433), channel_id=1, source_target_pairs={{0,1},{1,0},{2,3},{3,2},{4,5},{5,4},{6,7},{7,6},{8,9},{9,8},{10,11... | collective-permute-start | bytes 21512 | tf_op jit(solution)/shard_map/ppermute | solution.py:20
  253.1 0.9 copy-start.3
  253.1 1.2 copy-start.7
  253.1 1.3 copy-start.13
Sparse Core Ops, SparseCore 0:
  10.5 74.6 all-gather.5
  87.0 58.2 all-gather.7
  147.2 48.8 all-gather.9
  253.3 90.4 reduce-scatter.1
where the time goes:
time: 353 us; the launch traced here: 352 us
  blocking collectives  136 us (39%)
  waiting for transfers between devices  95.3 us (27%)
  matrix products  51.7 us (15%)
  local copies, waits for them, and re-layouts  31.7 us (9%)
  between operations  15 us (4%)
  other arithmetic  14.3 us (4%)
  starting transfers between devices  5.51 us (2%)
    reduce_scatter x1, waiting for transfers between devices, shards(): mine = lax.psum_scatter(terms, 'mp', scatter_dimension=1, tiled=True)  70.2 us
    unnamed x1, blocking collectives  69.3 us
    all_gather x1, blocking collectives, shards(): lax.all_gather(w_key, 'dp', axis=0, tiled=True)  26 us
    ppermute x6, waiting for transfers between devices, from_partner(): return lax.ppermute(block, axis, route)  24.4 us
    all_gather x1, blocking collectives, shards(): lax.all_gather(w_value, 'dp', axis=0, tiled=True)  24.1 us
    all_gather x1, blocking collectives, shards(): every_row = lax.all_gather(chosen, 'dp', axis=0, tiled=True)  16.2 us
    dot_general x4, matrix products, one_request(): jnp.einsum('gqd,gkd->gqk', queries, cached_keys, preferred_element_type=j...  14.5 us
    dot_general x4, matrix products, one_request(): jnp.einsum('gqk,gkd->gqd', probs_cache, cached_values, preferred_element_...  12.3 us
  transfers between devices with their start and end apart: 10, of which 4 were waited for; matrix products, arithmetic and copies ran while one was open for 24% of the time, Pallas kernels for 0%

commit v1 on v0

--- a/solution.py
+++ b/solution.py
@@ -67,7 +67,9 @@
     q_cols = w_query.shape[1]
     k_cols = w_key.shape[1]
     gathered, full_gain = (
-        lax.all_gather(hidden_in, "mp", axis=2, tiled=True),
+        jnp.concatenate(
+            lax.all_to_all(jnp.stack([hidden_in] * lax.axis_size("mp")), "mp", 0, 0), axis=2
+        ),
         lax.all_gather(norm_gain, "mp", axis=0, tiled=True),
     )
     widened = gathered.astype(jnp.float32)

time: 353 us -> 409 us (1.16)
  blocking collectives: 136 us -> 175 us
  starting transfers between devices: 5.51 us -> 12.7 us
  other arithmetic: 14.3 us -> 20.9 us
  local copies, waits for them, and re-layouts: 31.7 us -> 37.2 us
    unnamed x1, blocking collectives: 69.3 us -> 118 us
    convert_element_type x0 -> x2, local copies, waits for them, and re-layouts: none -> 17.8 us  [shards(): widened = gathered.astype(jnp.float32)]
    all_gather x1 -> x0, local copies, waits for them, and re-layouts: 11.3 us -> none  [shards(): lax.all_gather(hidden_in, 'mp', axis=2, tiled=True)]
    all_to_all x0 -> x1, starting transfers between devices: none -> 7.62 us  [shards(): lax.all_to_all(jnp.stack([hidden_in] * lax.axis_size('mp')), 'mp', 0, 0)]
    all_gather x1, blocking collectives: 24.1 us -> 17.7 us  [shards(): lax.all_gather(w_value, 'dp', axis=0, tiled=True)]
    unnamed x36 -> x41, local copies, waits for them, and re-layouts: 11.3 us -> 6.74 us
  transfers between devices with their start and end apart: 10 -> 10, of which waited for: 4 -> 5; matrix products, arithmetic and copies ran while one was open for 24% -> 24% of each run, Pallas kernels for 0% -> 0%
where the time goes in v1:
time: 409 us; the launch traced here: 408 us
  blocking collectives  175 us (43%)
  waiting for transfers between devices  93.2 us (23%)
  matrix products  50.9 us (12%)
  local copies, waits for them, and re-layouts  37.2 us (9%)
  other arithmetic  20.9 us (5%)
  between operations  15 us (4%)
  starting transfers between devices  12.7 us (3%)
    unnamed x1, blocking collectives  118 us
    reduce_scatter x1, waiting for transfers between devices, shards(): mine = lax.psum_scatter(terms, 'mp', scatter_dimension=1, tiled=True)  68.2 us
    ppermute x6, waiting for transfers between devices, from_partner(): return lax.ppermute(block, axis, route)  24.2 us
    all_gather x1, blocking collectives, shards(): lax.all_gather(w_key, 'dp', axis=0, tiled=True)  22.9 us
    convert_element_type x2, local copies, waits for them, and re-layouts, shards(): widened = gathered.astype(jnp.float32)  17.8 us
    all_gather x1, blocking collectives, shards(): lax.all_gather(w_value, 'dp', axis=0, tiled=True)  17.7 us
    all_gather x1, blocking collectives, shards(): every_row = lax.all_gather(chosen, 'dp', axis=0, tiled=True)  16.5 us
    dot_general x4, matrix products, one_request(): jnp.einsum('gqd,gkd->gqk', queries, cached_keys, preferred_element_type=j...  14 us
  transfers between devices with their start and end apart: 10, of which 5 were waited for; matrix products, arithmetic and copies ran while one was open for 24% of the time, Pallas kernels for 0%

profile of v1, /device:TPU:2, one launch (start us, length us, event | category | flops | bytes accessed | tf_op | source)
XLA Modules:
  0.0 408.1 jit_solution(7343243048219357958)
XLA Ops:
  7.2 0.7 all-gather.5.cloned.1.call-update
  7.9 3.5 stack.4
  11.4 7.6 %all-to-all-start = ((bf16[16,4,64,448]{3,2,1,0:T(8,128)(2,1)}), bf16[16,4,64,448]{3,2,1,0:T(8,128)(2,1)}, u32[]{:S(2)}, u32[]{:S(2)}) async-start(bf16[16,4,64,448]{3,2,1,0:T(8,128)(2,1)} %stack.4), calls=%async_computation | async-start | bytes 8388608 | tf_op jit(solution)/shard_map/all_to_all | solution.py:71
  19.1 1.0 copy.127
  20.2 0.6 dynamic-slice.1
  21.8 117.9 %all-reduce = bf16[7168]{0:T(1024)(128)(2,1)S(1)} all-reduce(bf16[7168]{0:T(1024)(128)(2,1)S(1)} %dynamic-update-slice), channel_id=1, replica_groups=mesh['dp'=16,'mp'=16] {'mp'}, use_global_device_ids=true, to_apply=%add | all-reduce | flops 7168 | bytes 28672
  139.7 22.9 %all-gather = bf16[16,448,64]{1,2,0:T(8,128)(2,1)S(1)} all-gather(bf16[1,448,64]{1,2,0:T(8,128)(2,1)S(1)} %bitcast.153), channel_id=1, replica_groups=mesh['dp'=16,'mp'=16] {'dp'}, dimensions={0}, use_global_device_ids=true | all-gather | bytes 974848 | tf_op jit(solution)/shard_map/all_gather | solution.py:83
  162.6 0.6 copy.110
  163.2 1.2 reshape.592
  164.4 17.7 %all-gather.1 = bf16[16,448,64]{1,2,0:T(8,128)(2,1)S(1)} all-gather(bf16[1,448,64]{1,2,0:T(8,128)(2,1)S(1)} %bitcast.154), channel_id=1, replica_groups=mesh['dp'=16,'mp'=16] {'dp'}, dimensions={0}, use_global_device_ids=true | all-gather | bytes 974848 | tf_op jit(solution)/shard_map/all_gather | solution.py:84
  182.1 0.6 copy.117
  182.7 1.2 reshape.594
  185.8 0.5 fusion.40
  186.3 0.8 pad_maximum_fusion
  187.1 3.4 convert_bitcast_fusion
  190.5 8.1 %copy.104 = f32[4,64,16,448]{3,2,1,0:T(8,128)} copy(f32[4,64,16,448]{3,1,0,2:T(8,128)S(1)} %convert_bitcast_fusion) | data formatting | bytes 14680064 | tf_op jit(solution)/shard_map/convert_element_type | solution.py:75
  198.6 9.7 %reshape.566 = f32[256,7168]{1,0:T(8,128)} reshape(f32[4,64,16,448]{3,2,1,0:T(8,128)} %copy.104) | data formatting | bytes 14680064 | tf_op jit(solution)/shard_map/convert_element_type | solution.py:75
  208.3 3.2 fusion.22
  211.6 4.1 multiply_convert_fusion
  215.6 1.2 convolution_convert_fusion.2
  217.0 0.4 copy-done.1
  217.4 1.2 convolution_convert_fusion.1
  218.9 1.7 collective-permute-start.2
  221.4 7.0 %convolution_convert_fusion = bf16[256,448]{0,1:T(8,128)(2,1)S(1)} fusion(bf16[256,7168]{1,0:T(8,128)(2,1)} %copy-done.1, bf16[7168,448]{1,0:T(8,128)(2,1)} %all-gather.5.cloned.1.call-done), kind=kOutput, calls=%fused_computation.40 | convolution fusion | flops 1644281856 | bytes 10321920 | tf_op jit(solution)/shard_map/dot_general | solution.py:87
  228.7 0.4 fusion.34
  229.2 0.7 fusion.36
  230.0 5.6 %collective-permute-done = bf16[256,448]{0,1:T(8,128)(2,1)S(1)} collective-permute-done((bf16[256,448]{0,1:T(8,128)(2,1)S(1)}, bf16[256,448]{0,1:T(8,128)(2,1)S(1)}, u32[]{:S(2)}, u32[]{:S(2)}) %collective-permute-start) | collective-permute-done | bytes 229408 | tf_op jit(solution)/shard_map/ppermute | solution.py:20
  236.6 0.5 copy-done.4
  237.1 0.5 fusion.26
  237.7 42.0 %while.16 = (s32[]{:T(128)}, f32[4,1,448]{2,1,0:T(1,128)S(1)}, f32[4,1,448]{2,1,0:T(1,128)S(1)}, f32[4,1,448,128]{3,2,1,0:T(8,128)S(1)}, s32[4]{0:T(128)S(1)}, /...) while((s32[]{:T(128)}, f32[4,1,448]{2,1,0:T(1,128)S(1)}, ...), condition=%wide.region_7.8_spmd, body=%wide.region_2.7_spmd.sunk | while | flops 496694400 | bytes 28287568 | solution.py:155
  238.0 0.6 dynamic_slice.100
  239.3 3.5 fusion.77
  243.3 1.1 fusion.79
  244.4 3.1 fusion.80
  247.6 0.8 convert_reduce_fusion.4
  248.5 0.6 dynamic_slice.100
  249.7 3.5 fusion.77
  253.8 1.1 fusion.79
  254.9 3.1 fusion.80
  258.0 0.8 convert_reduce_fusion.4
  258.9 0.6 dynamic_slice.100
  260.2 3.5 fusion.77
  264.2 1.1 fusion.79
  265.3 3.1 fusion.80
  268.5 0.8 convert_reduce_fusion.4
  269.3 0.6 dynamic_slice.100
  270.6 3.5 fusion.77
  274.7 1.1 fusion.79
  275.8 3.1 fusion.80
  278.9 0.8 convert_reduce_fusion.4
  279.8 0.8 collective-permute-start.4
  280.6 1.3 collective-permute-start.3
  281.9 0.7 collective-permute-start.5
  282.7 18.3 %collective-permute-done.3 = f32[4,1,448]{2,1,0:T(1,128)S(1)} collective-permute-done((f32[4,1,448]{2,1,0:T(1,128)S(1)}, f32[4,1,448]{2,1,0:T(1,128)S(1)}, u32[]{:S(2)}, u32[]{:S(2)}) %collective-permute-start.3) | collective-permute-done | bytes 7200 | tf_op jit(solution)/shard_map/ppermute | solution.py:20
  301.2 0.9 divide_convert_fusion
  302.6 8.3 %fusion.28 = f32[256,7168]{0,1:T(8,128)} fusion(bf16[448,7168]{0,1:T(8,128)(2,1)} %all-gather.7.cloned.1.call-done, bf16[256,896]{1,0:T(8,128)(2,1)S(1)} %bitcast.145, s32[]{:T(128)S(6)} %select_n.115, bf16[256]{0:T(256)(128)(2,1)S(1)} %mul.208), kind=kOutput, calls=%fused_computation.62 | convolution fusion | flops 1644625920 | bytes 14025220 | tf_op jit(solution)/shard_map/dot_general | solution.py:175
  310.8 0.6 copy-done.8
  313.0 0.7 gather_fusion.1
  313.8 16.5 %all_gather.23 = bf16[64,8,2,64]{3,1,2,0:T(8,128)(2,1)S(1)} all-gather(bf16[4,8,2,64]{3,1,2,0:T(8,128)(2,1)S(1)} %copy_select_fusion), channel_id=1, replica_groups=mesh['dp'=16,'mp'=16] {'dp'}, dimensions={0}, use_global_device_ids=true | all-gather | bytes 139264 | tf_op jit(solution)/shard_map/all_gather | solution.py:193
  330.2 0.6 gather_fusion
  330.9 0.6 copy.132
  331.5 68.2 %reduce-scatter.2.cloned.1.call-done = f32[256,448]{0,1:T(8,128)} async-done(((f32[256,7168]{0,1:T(8,128)}), f32[256,448]{0,1:T(8,128)}) %reduce-scatter.2.cloned.1.call-update) | async-done | bytes 458768 | tf_op jit(solution)/shard_map/reduce_scatter | solution.py:180
  399.7 1.1 add_convert_fusion
  400.8 0.8 copy.129
  (157 shorter events, 9.7 us)
Async XLA Ops:
  7.2 214.2 %all-gather.5.cloned.1.call-start = ((), (), s32[]{:S(2)}) async-start(), calls=%async_computation.2 | async-start | bytes 7798784 | tf_op jit(solution)/shard_map/all_gather | solution.py:82
  11.4 7.7 %copy-start.5 = (bf16[448,448]{1,0:T(8,128)(2,1)S(1)}, bf16[448,448]{1,0:T(8,128)(2,1)}, u32[]{:S(2)}) copy-start(bf16[448,448]{1,0:T(8,128)(2,1)} %param.20) | copy-start | bytes 1204228
  11.4 8.8 %copy-start.16 = (u32[256]{0:T(256)S(1)}, u32[256]{0:T(256)}, u32[]{:S(2)}) copy-start(u32[256]{0:T(256)} %constant.151) | copy-start | bytes 3076
  11.4 10.1 %copy-start.11 = (bf16[448]{0:T(512)(128)(2,1)S(1)}, bf16[448]{0:T(512)(128)(2,1)}, u32[]{:S(2)}) copy-start(bf16[448]{0:T(512)(128)(2,1)} %param.16) | copy-start | bytes 2692
  11.4 128.3 %copy-start.6 = (bf16[448,64]{0,1:T(8,128)(2,1)S(1)}, bf16[448,64]{0,1:T(8,128)(2,1)}, u32[]{:S(2)}) copy-start(bf16[448,64]{0,1:T(8,128)(2,1)} %param.18) | copy-start | bytes 172036
  11.4 175.7 %all-to-all-start = ((bf16[16,4,64,448]{3,2,1,0:T(8,128)(2,1)}), bf16[16,4,64,448]{3,2,1,0:T(8,128)(2,1)}, u32[]{:S(2)}, u32[]{:S(2)}) async-start(bf16[16,4,64,448]{3,2,1,0:T(8,128)(2,1)} %stack.4), calls=%async_computation | async-start | bytes 8388608 | tf_op jit(solution)/shard_map/all_to_all | solution.py:71
  19.0 145.3 %copy-start.12 = (s32[4]{0:T(128)S(1)}, s32[4]{0:T(128)}, u32[]{:S(2)}) copy-start(s32[4]{0:T(128)} %param.23) | copy-start | bytes 52
  19.0 145.4 %copy-start.7 = (bf16[448,64]{0,1:T(8,128)(2,1)S(1)}, bf16[448,64]{0,1:T(8,128)(2,1)}, u32[]{:S(2)}) copy-start(bf16[448,64]{0,1:T(8,128)(2,1)} %param.19) | copy-start | bytes 172036
  19.1 283.5 %all-gather.7.cloned.1.call-start = ((), (), s32[]{:S(2)}) async-start(), calls=%async_computation.3 | async-start | bytes 7798784 | tf_op jit(solution)/shard_map/all_gather | solution.py:177
  20.1 379.6 %reduce-scatter.2.cloned.1.call-start = ((), (), s32[]{:S(2)}) async-start(), calls=%async_computation.4 | async-start | bytes 7798784 | tf_op jit(solution)/shard_map/reduce_scatter | solution.py:180
  163.2 20.7 %copy-start.10 = (s32[4,64]{1,0:T(4,128)S(1)}, s32[4,64]{1,0:T(4,128)}, u32[]{:S(2)}) copy-start(s32[4,64]{1,0:T(4,128)} %param.24) | copy-start | bytes 3076
  215.6 1.8 copy-start.1
  216.9 4.0 collective-permute-start.1
  218.9 10.2 %collective-permute-start.2 = (bf16[256,64]{0,1:T(8,128)(2,1)S(1)}, bf16[256,64]{0,1:T(8,128)(2,1)S(1)}, u32[]{:S(2)}, u32[]{:S(2)}) collective-permute-start(bf16[256,64]{0,1:T(8,128)(2,1)S(1)} %convolution_convert_fusion.1), channel_id=1, source_target_pairs={{0,1},{1,0},{2,3},{3,2},{4,5},{5,4},{6,7},{7,6},{8,9},{9,8},{10,11... | collective-permute-start | bytes 98312 | tf_op jit(solution)/shard_map/ppermute | solution.py:20
  228.4 7.2 %collective-permute-start = (bf16[256,448]{0,1:T(8,128)(2,1)S(1)}, bf16[256,448]{0,1:T(8,128)(2,1)S(1)}, u32[]{:S(2)}, u32[]{:S(2)}) collective-permute-start(bf16[256,448]{0,1:T(8,128)(2,1)S(1)} %convolution_convert_fusion), channel_id=1, source_target_pairs={{0,1},{1,0},{2,3},{3,2},{4,5},{5,4},{6,7},{7,6},{8,9},{9,8},{10,11... | collective-permute-start | bytes 688136 | tf_op jit(solution)/shard_map/ppermute | solution.py:20
  236.2 0.9 copy-start.4
  236.2 1.5 copy-start.3
  236.6 1.1 copy-start.13
  237.7 44.9 %copy-start.9 = (s32[4,64]{1,0:T(4,128)S(1)}, s32[4,64]{1,0:T(4,128)}, u32[]{:S(2)}) copy-start(s32[4,64]{1,0:T(4,128)} %param.25) | copy-start | bytes 3076
  243.1 4.5 %copy-start = (f32[448,2048]{1,0:T(8,128)S(1)}, f32[448,2048]{1,0:T(8,128)}, u32[]{:S(2)}) copy-start(f32[448,2048]{1,0:T(8,128)} %get-tuple-element.336) | copy-start | bytes 11010052 | tf_op jit(solution)/shard_map/while
  244.4 4.0 copy-start.14
  253.6 4.5 %copy-start = (f32[448,2048]{1,0:T(8,128)S(1)}, f32[448,2048]{1,0:T(8,128)}, u32[]{:S(2)}) copy-start(f32[448,2048]{1,0:T(8,128)} %get-tuple-element.336) | copy-start | bytes 11010052 | tf_op jit(solution)/shard_map/while
  254.9 4.0 copy-start.14
  264.0 4.5 %copy-start = (f32[448,2048]{1,0:T(8,128)S(1)}, f32[448,2048]{1,0:T(8,128)}, u32[]{:S(2)}) copy-start(f32[448,2048]{1,0:T(8,128)} %get-tuple-element.336) | copy-start | bytes 11010052 | tf_op jit(solution)/shard_map/while
  265.3 4.0 copy-start.14
  274.4 4.5 %copy-start = (f32[448,2048]{1,0:T(8,128)S(1)}, f32[448,2048]{1,0:T(8,128)}, u32[]{:S(2)}) copy-start(f32[448,2048]{1,0:T(8,128)} %get-tuple-element.336) | copy-start | bytes 11010052 | tf_op jit(solution)/shard_map/while
  275.8 4.0 copy-start.14
  279.8 21.4 %collective-permute-start.4 = (f32[4,1,448,128]{3,2,1,0:T(8,128)S(1)}, f32[4,1,448,128]{3,2,1,0:T(8,128)S(1)}, u32[]{:S(2)}, u32[]{:S(2)}) collective-permute-start(f32[4,1,448,128]{3,2,1,0:T(8,128)S(1)} %get-tuple-element.417), channel_id=1, source_target_pairs={{0,1},{1,0},{2,3},{3,2},{4,5},{5,4},{6,7},{7,6},{8,9},{9,8},{10,11... | collective-permute-start | bytes 2752520 | tf_op jit(solution)/shard_map/ppermute | solution.py:20
  280.6 20.5 %collective-permute-start.3 = (f32[4,1,448]{2,1,0:T(1,128)S(1)}, f32[4,1,448]{2,1,0:T(1,128)S(1)}, u32[]{:S(2)}, u32[]{:S(2)}) collective-permute-start(f32[4,1,448]{2,1,0:T(1,128)S(1)} %get-tuple-element.415), channel_id=1, source_target_pairs={{0,1},{1,0},{2,3},{3,2},{4,5},{5,4},{6,7},{7,6},{8,9},{9,8},{10,11... | collective-permute-start | bytes 21512 | tf_op jit(solution)/shard_map/ppermute | solution.py:20
  281.9 19.2 %collective-permute-start.5 = (f32[4,1,448]{2,1,0:T(1,128)S(1)}, f32[4,1,448]{2,1,0:T(1,128)S(1)}, u32[]{:S(2)}, u32[]{:S(2)}) collective-permute-start(f32[4,1,448]{2,1,0:T(1,128)S(1)} %get-tuple-element.416), channel_id=1, source_target_pairs={{0,1},{1,0},{2,3},{3,2},{4,5},{5,4},{6,7},{7,6},{8,9},{9,8},{10,11... | collective-permute-start | bytes 21512 | tf_op jit(solution)/shard_map/ppermute | solution.py:20
  310.8 0.7 copy-start.8
  310.8 1.0 copy-start.2
  310.8 1.2 copy-start.15
Sparse Core Ops, SparseCore 0:
  9.8 53.9 all-gather.4
  65.7 49.4 all-gather.6
  311.0 88.6 reduce-scatter.1
